TPU v7x, 128 devices: a whole 4x4x4 slice. The times are simulated.
128 devices in a mesh: freq: 8 (over x, core), slab: 16 (over y, z).
Axes of the slice: x: 4, y: 4, z: 4, core: 2. Of those that a mesh axis runs over, the one named last changes fastest.
Arguments:
- traces: bfloat16 [393216, 2048], P(('freq', 'slab')), may hold values from -6 to 6
- trace_counts: int32 [128, 8], P(('freq', 'slab')), may hold values from 1 to 512, 3072 in all within a row
- aperture_start: int32 [1024], P(('freq', 'slab')), may hold values from 0 to 511
- shot_position: int32 [1024], P(('freq', 'slab')), may hold values from 0 to 4095
- rec_slot: int32 [512], replicated, may hold values from 0 to 767, as said below
Outputs:
- encoded: bfloat16 [768, 256, 256], P('slab', 'freq')
Inputs may be any that keep to these rules, and one draw needn't show every extreme that they name: `rec_slot`: distinct receivers have distinct slots. No depth slab owns more than 48 receivers, at least one owns exactly 48, and slots 0 and 767 are always used.
All inputs are finite; a program needn't handle non-finite values.
Results may differ from a plain program's by a relative error of at most 0.0062.
Values may be sent and summed in bfloat16 or wider, within the bound.
No kernel may reach another device: no remote copies, remote signals or barrier semaphores. Data moves between devices by JAX's collectives and lax.ppermute only.
A program may use at most 192 MiB of HBM per device.

v0:
```python
import math
import jax
import jax.numpy as jnp
from jax import lax
from jax.sharding import PartitionSpec as P

NT = 2048
FREQUENCY_COUNT = 256
F0 = 8
RAY_PARAM_COUNT = 128
NREC = 512
RDIV = 16


def dft_factors(freq_bins, samples):
    sample_index = jnp.arange(samples, dtype=jnp.int32)
    phase_index = jnp.remainder(sample_index[:, None] * freq_bins[None, :], samples)
    angle_rad = phase_index.astype(jnp.float32) * (2.0 * math.pi / samples)
    factor = 1.0 / math.sqrt(samples)
    return (
        (jnp.cos(angle_rad) * factor).astype(jnp.bfloat16),
        (-jnp.sin(angle_rad) * factor).astype(jnp.bfloat16),
    )


def phase_blocks(freq_bins, positions, total_shots):
    ray_offset = jnp.arange(RAY_PARAM_COUNT, dtype=jnp.int32) - RAY_PARAM_COUNT // 2
    period = NT * RDIV
    product = (
        freq_bins[:, None, None, None]
        * ray_offset[None, None, None, :]
        * positions[None, :, :, None]
    )
    angle_rad = jnp.remainder(product, period).astype(jnp.float32) * (2.0 * math.pi / period)
    factor = 1.0 / math.sqrt(total_shots)
    cosine = (jnp.cos(angle_rad) * factor).astype(jnp.bfloat16)
    sine_part = (jnp.sin(angle_rad) * factor).astype(jnp.bfloat16)
    upper_half = jnp.concatenate([cosine, -sine_part], axis=3)
    lower_half = jnp.concatenate([sine_part, cosine], axis=3)
    stacked = jnp.stack([upper_half, lower_half], axis=2)
    return stacked.reshape(
        freq_bins.shape[0], positions.shape[0] * 2 * positions.shape[1], 2 * RAY_PARAM_COUNT
    )


def frequency_spectra(transform, traces):
    return lax.dot_general(
        transform, traces, (((0,), (1,)), ((), ())), preferred_element_type=jnp.float32
    ).astype(jnp.bfloat16)


def receiver_index(counts, starts, row_total, shot_total):
    shot_count = counts.shape[0]
    by_source = counts.reshape(shot_count // shot_total, shot_total)
    inclusive = jnp.cumsum(by_source, axis=1)
    source_base = (jnp.arange(shot_count // shot_total, dtype=jnp.int32) * row_total)[:, None]
    begins = (source_base + inclusive - by_source).reshape(shot_count)
    receivers = jnp.arange(NREC, dtype=jnp.int32)
    offset = jnp.remainder(receivers[None, :] - starts[:, None], NREC)
    valid = offset < counts[:, None]
    picks = jnp.where(valid, begins[:, None] + offset, 0)
    return (picks, valid)


def slot_matrix(rec_slot, slot_count):
    return (rec_slot[:, None] == jnp.arange(slot_count, dtype=jnp.int32)[None, :]).astype(
        jnp.bfloat16
    )


def slot_grid(
    owned_spectra, counts, starts, row_total, shot_total, slot_count, freq_block, rec_slot
):
    picks, valid = receiver_index(counts, starts, row_total, shot_total)
    shot_count = counts.shape[0]
    picked = jnp.take(owned_spectra, picks.reshape(-1), axis=1)
    picked = picked.reshape(2, freq_block, shot_count, NREC)
    picked = jnp.where(valid[None, None, :, :], picked, jnp.zeros((), jnp.bfloat16))
    lattice = jnp.einsum(
        "rs,cfhr->sfch",
        slot_matrix(rec_slot, slot_count),
        picked,
        preferred_element_type=jnp.float32,
    )
    return lattice.astype(jnp.bfloat16).reshape(slot_count, freq_block, 2 * shot_count)


def on_device(traces, trace_counts, aperture_start, shot_position, rec_slot):
    row_total, samples = traces.shape
    shot_total = trace_counts.shape[1]
    freq_groups = lax.axis_size("freq")
    slab_groups = lax.axis_size("slab")
    freq_block = FREQUENCY_COUNT // freq_groups
    slot_cap = 3 * NREC // (2 * slab_groups)
    slot_count = slot_cap * slab_groups
    all_shots = shot_total * freq_groups * slab_groups
    column = jnp.arange(2 * FREQUENCY_COUNT, dtype=jnp.int32)
    owner_block = column // (2 * freq_block)
    within = column % (2 * freq_block)
    column_bins = F0 + owner_block * freq_block + within % freq_block
    cosine_table, sine_table = dft_factors(column_bins, samples)
    transform = jnp.where((within // freq_block == 0)[None, :], cosine_table, sine_table)
    local_bins = F0 + lax.axis_index("freq") * freq_block + jnp.arange(freq_block, dtype=jnp.int32)
    own_counts = trace_counts[0]
    spectra = frequency_spectra(transform, traces)
    holder_counts, holder_starts, holder_positions = (
        lax.all_gather(own_counts, "freq", axis=0, tiled=True),
        lax.all_gather(aperture_start, "freq", axis=0, tiled=True),
        lax.all_gather(shot_position, "freq", axis=0, tiled=True),
    )
    owned_spectra = lax.all_to_all(spectra, "freq", split_axis=0, concat_axis=1, tiled=True)
    filled_lattice = slot_grid(
        owned_spectra,
        holder_counts,
        holder_starts,
        row_total,
        shot_total,
        slot_count,
        freq_block,
        rec_slot,
    )
    phases = phase_blocks(local_bins, holder_positions[None, :], all_shots)
    summed = lax.psum_scatter(
        jnp.einsum("xfs,fsq->xfq", filled_lattice, phases, preferred_element_type=jnp.float32),
        "slab",
        scatter_dimension=0,
        tiled=True,
    )
    return summed.astype(jnp.bfloat16)


def solution(mesh):
    return jax.shard_map(
        on_device,
        mesh=mesh,
        in_specs=(
            P(("freq", "slab"), None),
            P(("freq", "slab"), None),
            P(("freq", "slab")),
            P(("freq", "slab")),
            P(),
        ),
        out_specs=P("slab", "freq", None),
        check_vma=False,
    )
```

profile of v0, /device:TPU:1, one launch (start us, length us, event | category | flops | bytes accessed | tf_op | source)
XLA Modules:
  0.0 433.4 jit_solution(2946370972484755948)
XLA Ops:
  6.6 28.7 %convolution_convert_fusion = bf16[512,3072]{1,0:T(8,128)(2,1)} fusion(bf16[3072,2048]{1,0:T(8,128)(2,1)} %param.5, s32[512]{0:T(512)S(1)} %fusion.42, pred[512]{0:T(512)(128)(4,1)S(1)} %fusion.38), kind=kOutput, calls=%fused_computation.6 | convolution fusion | flops 6464995328 | bytes 15731200 | tf_op jit(solution)/shard_map/dot_general | solution.py:47
  35.3 0.0 copy-start.4
  35.3 0.0 copy-start.1
  35.3 0.0 copy-start.2
  35.3 0.0 copy-start.3
  35.3 6.1 %all-to-all-start = ((bf16[8,64,3072]{2,1,0:T(8,128)(2,1)}), bf16[8,64,3072]{2,1,0:T(8,128)(2,1)}, u32[]{:S(2)}, u32[]{:S(2)}) async-start(bf16[8,64,3072]{2,1,0:T(8,128)(2,1)} %bitcast.5), calls=%async_computation | async-start | bytes 6291456 | tf_op jit(solution)/shard_map/all_to_all | solution.py:111
  41.4 0.0 reduce-scatter.2.cloned.1.call-start
  41.4 0.0 copy-done.4
  41.4 0.6 dynamic-slice
  42.7 0.0 copy-done.1
  42.7 0.1 bitcast_dynamic-update-slice_fusion
  42.8 0.0 copy-done.2
  42.8 0.2 dynamic-update-slice
  43.0 0.0 copy-done.3
  43.0 0.2 dynamic-update-slice.1
  43.3 37.4 %all-reduce.3 = (s32[64]{0:T(128)S(1)}, s32[64]{0:T(128)S(1)}, s32[64]{0:T(128)S(1)}) all-reduce(s32[64]{0:T(128)S(1)} %dynamic-update-slice, s32[64]{0:T(128)S(1)} %bitcast_dynamic-update-slice_fusion, s32[64]{0:T(128)S(1)} %dynamic-update-slice.1), channel_id=1, replica_groups=mesh['freq'=8,'slab'=16] {'freq'}, use_global_device_ids=true, to_apply=%add | all-reduce | flops 192 | bytes 1536
  80.7 0.1 reshape.351
  80.8 0.2 reduce_window_sum.11
  81.0 0.1 broadcast_add_fusion
  81.0 0.1 add.184
  81.1 0.1 broadcast_bitcast_fusion.1
  81.2 0.1 copy.29
  81.3 0.1 fusion.33
  81.4 0.1 copy.27
  81.6 0.1 copy.28
  81.7 0.6 compare_select_fusion
  82.3 0.1 broadcast_multiply_fusion
  82.4 4.2 fusion.37
  86.6 4.6 %multiply_convert_fusion.3 = (bf16[32,1,64,128]{3,2,0,1:T(8,128)(2,1)S(1)}, bf16[32,1,64,128]{3,2,0,1:T(8,128)(2,1)S(1)}) fusion(s32[64]{0:T(128)S(1)} %get-tuple-element.5, s32[32,128]{1,0:T(8,128)S(1)} %broadcast_multiply_fusion), kind=kLoop, calls=%fused_computation.43 | loop fusion | flops 4718592 | bytes 1065216 | tf_op jit(solution)/shard_map/convert_element_type | solution.py:37
  91.2 0.3 maximum_bitcast_fusion
  91.6 0.2 pad_maximum_fusion
  91.8 0.1 copy.17
  91.9 0.2 broadcast_compare_fusion
  92.1 0.0 all-to-all-done
  92.1 6.6 %copy.18 = bf16[64,8,3072]{0,2,1:T(8,128)(2,1)} copy(bf16[64,8,3072]{2,0,1:T(8,128)(2,1)} %bitcast.6) | data formatting | bytes 6291456 | tf_op jit(solution)/shard_map/all_to_all | solution.py:111
  98.7 113.7 %gather_fusion = bf16[32768,64]{1,0:T(8,128)(2,1)} fusion(bf16[64,24576]{0,1:T(8,128)(2,1)} %bitcast.53, s32[32768]{0:T(1024)S(1)} %broadcast_clamp_fusion), kind=kCustom, calls=%fused_computation | custom fusion | bytes 8519680 | tf_op jit(solution)/shard_map/jit(_take)/gather | solution.py:76
  212.4 8.6 %copy.19 = bf16[64,32768]{1,0:T(8,128)(2,1)} copy(bf16[64,32768]{0,1:T(8,128)(2,1)} %bitcast.55) | data formatting | bytes 8388608 | tf_op jit(solution)/shard_map/jit(_take)/gather | solution.py:76
  221.1 0.0 copy-start
  221.1 3.8 copy.30
  224.9 0.0 copy-done
  224.9 5.8 %convert_bitcast_fusion = bf16[768,32,2,64]{0,3,1,2:T(8,128)(2,1)} fusion(pred[64,512]{1,0:T(8,128)(4,1)S(1)} %get-tuple-element.13, pred[64,512]{1,0:T(8,128)(4,1)S(1)} %get-tuple-element.12, s32[512]{0:T(512)S(1)} %copy-done, bf16[2,32,64,512]{3,2,1,0:T(8,128)(2,1)S(1)} %bitcast.58), kind=kOutput, calls=%fused_computation.2 | convolution fusion | flops 3228958720 | bytes 10553344 | tf_op jit(solution)/shard_map/rs,cfhr->sfch/dot_general | solution.py:79
  230.7 3.2 copy.20
  233.9 10.1 %convolution_bitcast_fusion = f32[768,32,256]{0,2,1:T(8,128)} fusion(bf16[32,128,256]{2,1,0:T(8,128)(2,1)S(1)} %bitcast.57, bf16[768,32,128]{0,2,1:T(8,128)(2,1)S(1)} %bitcast.54), kind=kOutput, calls=%fused_computation.1 | convolution fusion | flops 1610612736 | bytes 33554432 | tf_op jit(solution)/shard_map/xfs,fsq->xfq/dot_general | solution.py:124
  243.9 25.1 %copy.23 = f32[768,32,256]{2,1,0:T(8,128)} copy(f32[768,32,256]{0,2,1:T(8,128)} %convolution_bitcast_fusion) | data formatting | bytes 50331648 | tf_op jit(solution)/shard_map/xfs,fsq->xfq/transpose | solution.py:124
  269.0 0.0 reduce-scatter.2.cloned.1.call-update
  269.0 155.1 %reduce-scatter.2.cloned.1.call-done = f32[48,32,256]{2,1,0:T(8,128)} async-done(((f32[768,32,256]{2,1,0:T(8,128)}), f32[48,32,256]{2,1,0:T(8,128)}) %reduce-scatter.2.cloned.1.call-update) | async-done | bytes 1572880 | tf_op jit(solution)/shard_map/reduce_scatter | solution.py:123
  424.2 2.4 convert_element_type.76
  (10 shorter events, 0.1 us)
Async XLA Ops:
  35.3 6.2 %copy-start.4 = (u32[128]{0:T(128)S(1)}, u32[128]{0:T(128)}, u32[]{:S(2)}) copy-start(u32[128]{0:T(128)} %constant.147) | copy-start | bytes 1540
  35.3 7.4 %copy-start.1 = (s32[1,8]{1,0:T(1,128)S(1)}, s32[1,8]{1,0:T(1,128)}, u32[]{:S(2)}) copy-start(s32[1,8]{1,0:T(1,128)} %param.6) | copy-start | bytes 100
  35.3 7.5 %copy-start.2 = (s32[8]{0:T(128)S(1)}, s32[8]{0:T(128)}, u32[]{:S(2)}) copy-start(s32[8]{0:T(128)} %param.8) | copy-start | bytes 100
  35.3 7.8 %copy-start.3 = (s32[8]{0:T(128)S(1)}, s32[8]{0:T(128)}, u32[]{:S(2)}) copy-start(s32[8]{0:T(128)} %param.7) | copy-start | bytes 100
  35.3 56.8 %all-to-all-start = ((bf16[8,64,3072]{2,1,0:T(8,128)(2,1)}), bf16[8,64,3072]{2,1,0:T(8,128)(2,1)}, u32[]{:S(2)}, u32[]{:S(2)}) async-start(bf16[8,64,3072]{2,1,0:T(8,128)(2,1)} %bitcast.5), calls=%async_computation | async-start | bytes 6291456 | tf_op jit(solution)/shard_map/all_to_all | solution.py:111
  41.4 382.8 %reduce-scatter.2.cloned.1.call-start = ((), (), s32[]{:S(2)}) async-start(), calls=%async_computation.2 | async-start | bytes 26738688 | tf_op jit(solution)/shard_map/reduce_scatter | solution.py:123
  221.1 3.8 copy-start
Sparse Core Ops, SparseCore 0:
  269.2 154.9 reduce-scatter.1
where the time goes:
time: 434 us; the launch traced here: 433 us
  local copies, waits for them, and re-layouts  163 us (38%)
  waiting for transfers between devices  155 us (36%)
  matrix products  44.6 us (10%)
  blocking collectives  37.4 us (9%)
  between operations  14.2 us (3%)
  other arithmetic  12.9 us (3%)
  starting transfers between devices  6.13 us (1%)
    reduce_scatter x1, waiting for transfers between devices, on_device(): lax.psum_scatter(jnp.einsum('xfs,fsq->xfq', filled_lattice, phases, prefe...  155 us
    gather x2, local copies, waits for them, and re-layouts, slot_grid(): picked = jnp.take(owned_spectra, picks.reshape(-1), axis=1)  122 us
    unnamed x1, blocking collectives  37.4 us
    dot_general x1, matrix products, frequency_spectra(): lax.dot_general(transform, traces, (((0,), (1,)), ((), ())), preferred_el...  28.7 us
    transpose x1, local copies, waits for them, and re-layouts, on_device(): jnp.einsum('xfs,fsq->xfq', filled_lattice, phases, preferred_element_type...  25.1 us
    dot_general x1, matrix products, on_device(): jnp.einsum('xfs,fsq->xfq', filled_lattice, phases, preferred_element_type...  10.1 us
  transfers between devices with their start and end apart: 2, of which 1 were waited for; matrix products, arithmetic and copies ran while one was open for 3% of the time, Pallas kernels for 0%

commit v1 on v0

--- a/solution.py
+++ b/solution.py
@@ -108,7 +108,10 @@
         lax.all_gather(aperture_start, "freq", axis=0, tiled=True),
         lax.all_gather(shot_position, "freq", axis=0, tiled=True),
     )
-    owned_spectra = lax.all_to_all(spectra, "freq", split_axis=0, concat_axis=1, tiled=True)
+    owned_spectra = jnp.concatenate(
+        lax.all_to_all(jnp.stack(jnp.split(spectra, lax.axis_size("freq"), axis=0)), "freq", 0, 0),
+        axis=1,
+    )
     filled_lattice = slot_grid(
         owned_spectra,
         holder_counts,

time: 434 us -> 440 us (1.014)
  local copies, waits for them, and re-layouts: 163 us -> 169 us
    all_to_all x1 -> x0, local copies, waits for them, and re-layouts: 6.59 us -> none  [on_device(): lax.all_to_all(spectra, 'freq', split_axis=0, concat_axis=1, tiled=True)]
    reshape x0 -> x1, local copies, waits for them, and re-layouts: none -> 6.59 us  [on_device(): jnp.concatenate(lax.all_to_all(jnp.stack(jnp.split(spectra, lax.axis_size...]
    unnamed x22 -> x29, local copies, waits for them, and re-layouts: 5.45 us -> 10.9 us
where the time goes in v1:
time: 440 us; the launch traced here: 439 us
  local copies, waits for them, and re-layouts  169 us (38%)
  waiting for transfers between devices  155 us (35%)
  matrix products  43.6 us (10%)
  blocking collectives  37.4 us (8%)
  between operations  14.2 us (3%)
  other arithmetic  12.9 us (3%)
  starting transfers between devices  5.95 us (1%)
    reduce_scatter x1, waiting for transfers between devices, on_device(): lax.psum_scatter(jnp.einsum('xfs,fsq->xfq', filled_lattice, phases, prefe...  155 us
    gather x2, local copies, waits for them, and re-layouts, slot_grid(): picked = jnp.take(owned_spectra, picks.reshape(-1), axis=1)  122 us
    unnamed x1, blocking collectives  37.4 us
    dot_general x1, matrix products, frequency_spectra(): lax.dot_general(transform, traces, (((0,), (1,)), ((), ())), preferred_el...  27.8 us
    transpose x1, local copies, waits for them, and re-layouts, on_device(): jnp.einsum('xfs,fsq->xfq', filled_lattice, phases, preferred_element_type...  25.1 us
    unnamed x29, local copies, waits for them, and re-layouts  10.9 us
    dot_general x1, matrix products, on_device(): jnp.einsum('xfs,fsq->xfq', filled_lattice, phases, preferred_element_type...  10.1 us
  transfers between devices with their start and end apart: 2, of which 1 were waited for; matrix products, arithmetic and copies ran while one was open for 3% of the time, Pallas kernels for 0%

profile of v1, /device:TPU:1, one launch (start us, length us, event | category | flops | bytes accessed | tf_op | source)
XLA Modules:
  0.0 438.5 jit_solution(15303601024521184483)
XLA Ops:
  6.6 27.8 %convolution_convert_fusion = bf16[512,3072]{1,0:T(8,128)(2,1)S(1)} fusion(bf16[3072,2048]{1,0:T(8,128)(2,1)} %param.5, s32[512]{0:T(512)S(1)} %fusion.50, pred[512]{0:T(512)(128)(4,1)S(1)} %fusion.46), kind=kOutput, calls=%fused_computation.6 | convolution fusion | flops 6464995328 | bytes 15731200 | tf_op jit(solution)/shard_map/dot_general | solution.py:47
  34.3 0.8 fusion.38
  35.1 0.8 fusion.37
  35.9 0.8 fusion.36
  36.6 0.8 fusion.35
  37.4 0.8 fusion.34
  38.2 0.8 fusion.33
  39.0 0.8 fusion.32
  39.8 0.8 fusion.31
  40.6 5.9 %all-to-all-start = ((bf16[8,64,3072]{2,1,0:T(8,128)(2,1)}), bf16[8,64,3072]{2,1,0:T(8,128)(2,1)}, u32[]{:S(2)}, u32[]{:S(2)}) async-start(bf16[8,64,3072]{2,1,0:T(8,128)(2,1)} %fusion.31), calls=%async_computation | async-start | bytes 6291456 | tf_op jit(solution)/shard_map/all_to_all | solution.py:112
  46.5 0.0 reduce-scatter.2.cloned.1.call-start
  46.5 0.0 copy-done.4
  46.6 0.6 dynamic-slice
  47.8 0.0 copy-done.1
  47.8 0.1 bitcast_dynamic-update-slice_fusion
  47.9 0.0 copy-done.2
  47.9 0.2 dynamic-update-slice
  48.2 0.2 dynamic-update-slice.1
  48.4 37.4 %all-reduce.3 = (s32[64]{0:T(128)S(1)}, s32[64]{0:T(128)S(1)}, s32[64]{0:T(128)S(1)}) all-reduce(s32[64]{0:T(128)S(1)} %dynamic-update-slice, s32[64]{0:T(128)S(1)} %bitcast_dynamic-update-slice_fusion, s32[64]{0:T(128)S(1)} %dynamic-update-slice.1), channel_id=1, replica_groups=mesh['freq'=8,'slab'=16] {'freq'}, use_global_device_ids=true, to_apply=%add | all-reduce | flops 192 | bytes 1536
  85.8 0.1 reshape.354
  85.9 0.2 reduce_window_sum.11
  86.1 0.1 broadcast_add_fusion
  86.1 0.1 add.184
  86.2 0.1 broadcast_bitcast_fusion.1
  86.3 0.1 copy.32
  86.5 0.1 fusion.41
  86.5 0.1 copy.30
  86.7 0.1 copy.31
  86.8 0.6 compare_select_fusion
  87.5 0.1 broadcast_multiply_fusion
  87.5 4.2 fusion.45
  91.8 4.6 %multiply_convert_fusion.3 = (bf16[32,1,64,128]{3,2,0,1:T(8,128)(2,1)S(1)}, bf16[32,1,64,128]{3,2,0,1:T(8,128)(2,1)S(1)}) fusion(s32[64]{0:T(128)S(1)} %get-tuple-element.5, s32[32,128]{1,0:T(8,128)S(1)} %broadcast_multiply_fusion), kind=kLoop, calls=%fused_computation.43 | loop fusion | flops 4718592 | bytes 1065216 | tf_op jit(solution)/shard_map/convert_element_type | solution.py:37
  96.3 0.3 maximum_bitcast_fusion
  96.7 0.2 pad_maximum_fusion
  96.9 0.1 copy.17
  97.0 0.2 broadcast_compare_fusion
  97.2 0.0 all-to-all-done
  97.2 6.6 %copy.28 = bf16[64,8,3072]{0,2,1:T(8,128)(2,1)} copy(bf16[64,8,3072]{2,0,1:T(8,128)(2,1)} %bitcast.13) | data formatting | bytes 6291456 | tf_op jit(solution)/shard_map/reshape | solution.py:111
  103.8 113.7 %gather_fusion = bf16[32768,64]{1,0:T(8,128)(2,1)} fusion(bf16[64,24576]{0,1:T(8,128)(2,1)} %bitcast.84, s32[32768]{0:T(1024)S(1)} %broadcast_clamp_fusion), kind=kCustom, calls=%fused_computation | custom fusion | bytes 8519680 | tf_op jit(solution)/shard_map/jit(_take)/gather | solution.py:76
  217.6 8.6 %copy.20 = bf16[64,32768]{1,0:T(8,128)(2,1)} copy(bf16[64,32768]{0,1:T(8,128)(2,1)} %bitcast.86) | data formatting | bytes 8388608 | tf_op jit(solution)/shard_map/jit(_take)/gather | solution.py:76
  226.2 3.8 copy.33
  230.0 5.8 %convert_bitcast_fusion = bf16[768,32,2,64]{0,3,1,2:T(8,128)(2,1)} fusion(pred[64,512]{1,0:T(8,128)(4,1)S(1)} %get-tuple-element.13, pred[64,512]{1,0:T(8,128)(4,1)S(1)} %get-tuple-element.12, s32[512]{0:T(512)S(1)} %copy-done, bf16[2,32,64,512]{3,2,1,0:T(8,128)(2,1)S(1)} %bitcast.89), kind=kOutput, calls=%fused_computation.2 | convolution fusion | flops 3228958720 | bytes 10553344 | tf_op jit(solution)/shard_map/rs,cfhr->sfch/dot_general | solution.py:79
  235.8 3.2 copy.21
  239.0 10.1 %convolution_bitcast_fusion = f32[768,32,256]{0,2,1:T(8,128)} fusion(bf16[32,128,256]{2,1,0:T(8,128)(2,1)S(1)} %bitcast.88, bf16[768,32,128]{0,2,1:T(8,128)(2,1)S(1)} %bitcast.85), kind=kOutput, calls=%fused_computation.1 | convolution fusion | flops 1610612736 | bytes 33554432 | tf_op jit(solution)/shard_map/xfs,fsq->xfq/dot_general | solution.py:127
  249.1 25.1 %copy.24 = f32[768,32,256]{2,1,0:T(8,128)} copy(f32[768,32,256]{0,2,1:T(8,128)} %convolution_bitcast_fusion) | data formatting | bytes 50331648 | tf_op jit(solution)/shard_map/xfs,fsq->xfq/transpose | solution.py:127
  274.1 0.0 reduce-scatter.2.cloned.1.call-update
  274.2 155.1 %reduce-scatter.2.cloned.1.call-done = f32[48,32,256]{2,1,0:T(8,128)} async-done(((f32[768,32,256]{2,1,0:T(8,128)}), f32[48,32,256]{2,1,0:T(8,128)}) %reduce-scatter.2.cloned.1.call-update) | async-done | bytes 1572880 | tf_op jit(solution)/shard_map/reduce_scatter | solution.py:126
  429.3 2.4 convert_element_type.76
  (17 shorter events, 0.1 us)
Async XLA Ops:
  40.6 6.0 %copy-start.4 = (u32[128]{0:T(128)S(1)}, u32[128]{0:T(128)}, u32[]{:S(2)}) copy-start(u32[128]{0:T(128)} %constant.147) | copy-start | bytes 1540
  40.6 7.2 %copy-start.1 = (s32[1,8]{1,0:T(1,128)S(1)}, s32[1,8]{1,0:T(1,128)}, u32[]{:S(2)}) copy-start(s32[1,8]{1,0:T(1,128)} %param.6) | copy-start | bytes 100
  40.6 7.3 %copy-start.2 = (s32[8]{0:T(128)S(1)}, s32[8]{0:T(128)}, u32[]{:S(2)}) copy-start(s32[8]{0:T(128)} %param.8) | copy-start | bytes 100
  40.6 7.6 %copy-start.3 = (s32[8]{0:T(128)S(1)}, s32[8]{0:T(128)}, u32[]{:S(2)}) copy-start(s32[8]{0:T(128)} %param.7) | copy-start | bytes 100
  40.6 56.7 %all-to-all-start = ((bf16[8,64,3072]{2,1,0:T(8,128)(2,1)}), bf16[8,64,3072]{2,1,0:T(8,128)(2,1)}, u32[]{:S(2)}, u32[]{:S(2)}) async-start(bf16[8,64,3072]{2,1,0:T(8,128)(2,1)} %fusion.31), calls=%async_computation | async-start | bytes 6291456 | tf_op jit(solution)/shard_map/all_to_all | solution.py:112
  46.5 382.7 %reduce-scatter.2.cloned.1.call-start = ((), (), s32[]{:S(2)}) async-start(), calls=%async_computation.2 | async-start | bytes 26738688 | tf_op jit(solution)/shard_map/reduce_scatter | solution.py:126
  226.2 3.8 copy-start
Sparse Core Ops, SparseCore 0:
  274.3 154.9 reduce-scatter.1
